TPU v7x, 128 devices: a whole 4x4x4 slice. The times are simulated.
128 devices in a mesh: section: 2 (over core), node: 64 (over x, z, y).
Axes of the slice: x: 4, y: 4, z: 4, core: 2. Of those that a mesh axis runs over, the one named last changes fastest.
Arguments:
- node_latents: bfloat16 [2, 16384, 512], P(None, 'node'), may hold values from -6 to 6
- edge_latents: bfloat16 [2, 98304, 512], P(None, 'node'), may hold values from -6 to 6
- sender: int32 [98304], P('node'), may hold values from 0 to 511
- receiver: int32 [98304], P('node'), may hold values from 0 to 255
- send_up: int32 [8192], P('node'), may hold values from 0 to 255
- send_down: int32 [8192], P('node'), may hold values from 0 to 255
- edge_count: int32 [64], P('node'), may hold values from 512 to 1536, as said below
- w_edge_in: bfloat16 [4, 1536, 512], P('section'), may hold values from -0.15625 to 0.15625
- w_edge_out: bfloat16 [4, 512, 512], P('section'), may hold values from -0.25 to 0.25
- edge_gain: float32 [4, 512], P('section'), may hold values from 0.25 to 1.75
- w_node_in: bfloat16 [4, 1024, 512], P('section'), may hold values from -0.1875 to 0.1875
- w_node_out: bfloat16 [4, 512, 512], P('section'), may hold values from -0.25 to 0.25
- node_gain: float32 [4, 512], P('section'), may hold values from 0.25 to 1.75
Outputs:
- processed: bfloat16 [2, 16384, 512], P('section', 'node')
Inputs may be any that keep to these rules, and one draw needn't show every extreme that they name: `edge_count`: each shard has between 512 and 1536 live edge slots, and some shard has all 1536 live.
All inputs are finite; a program needn't handle non-finite values.
Results may differ from a plain program's by a relative error of at most 0.025.
Values may be sent and summed in bfloat16 or wider, within the bound.
A program may use at most 128 MiB of HBM per device.

v0:
```python
import functools

import jax
import jax.numpy as jnp
from jax import lax
from jax.experimental import pallas as pl
from jax.experimental.pallas import tpu as pltpu
from jax.sharding import PartitionSpec as P

D = 512
NV = 256
HALO = 128
E = 1536
L = 4
OWN = 2
TILE = 256
CHUNK = 128
MESH = pl.DeviceIdType.MESH

REC = D
LOC = REC + NV
HAL = LOC + NV
XW = HAL + 2 * HALO


def silu(x):
    half = 0.5 * x
    return half + half * jnp.tanh(half)


def residual_norm(base, update, gain):
    mean = jnp.mean(update, axis=-1, keepdims=True)
    centred = update - mean
    var = jnp.mean(centred * centred, axis=-1, keepdims=True)
    return (base.astype(jnp.float32) + gain * (centred * lax.rsqrt(var + 1e-05))).astype(jnp.bfloat16)


def dot(a, b):
    return jnp.dot(a, b, preferred_element_type=jnp.float32)


def kernel(
    n_node,
    node_in,
    edge_in,
    snd,
    rcv,
    upw,
    dnw,
    count,
    wei,
    weo,
    eg,
    wni,
    wno,
    ng,
    out,
    nodes,
    x,
    pre,
    oht,
    pick,
    wcat,
    w23,
    wo,
    ni,
    no,
    egs,
    ngs,
    halo,
    sendbuf,
    pre_node,
    in_sem,
    w_sem,
    ws_sem,
    h_recv,
    h_send,
):
    me = lax.axis_index("section")
    other = 1 - me
    at = lax.axis_index("node")
    above = lax.rem(at + 1, n_node)
    below = lax.rem(at + n_node - 1, n_node)

    copy_nodes = pltpu.make_async_copy(node_in.at[me], nodes, in_sem.at[0])
    copy_nodes.start()

    def pieces(j):
        k = OWN * me + j
        return [
            (wei.at[j, pl.ds(D, 2 * D)], w23.at[k]),
            (wei.at[j, pl.ds(0, D)], wcat.at[k, pl.ds(0, D)]),
            (weo.at[j], wo.at[k]),
            (wni.at[j], ni.at[k]),
            (wno.at[j], no.at[k]),
        ]

    own = []
    for j in range(OWN):
        for p, (src, dst) in enumerate(pieces(j)):
            own.append(pltpu.make_async_copy(src, dst, w_sem.at[OWN * me + j, p]))
    own.append(pltpu.make_async_copy(eg, egs.at[me], w_sem.at[me, 5]))
    own.append(pltpu.make_async_copy(ng, ngs.at[me], w_sem.at[me, 6]))
    for c in own[:5]:
        c.start()
    copy_edges = pltpu.make_async_copy(edge_in.at[me], x.at[:, pl.ds(0, D)], in_sem.at[1])
    copy_edges.start()
    for c in own[5:]:
        c.start()

    barrier = pltpu.get_barrier_semaphore()
    for target in ({"section": other}, {"node": above}, {"node": below}):
        pl.semaphore_signal(barrier, inc=1, device_id=target, device_id_type=MESH)
    pl.semaphore_wait(barrier, 3)

    remote = []
    for j in range(OWN):
        for p, (src, dst) in enumerate(pieces(j)):
            remote.append((src, dst, ws_sem.at[j, p], w_sem.at[OWN * me + j, p]))
    remote.insert(3, (eg, egs.at[me], ws_sem.at[0, 5], w_sem.at[me, 5]))
    remote.insert(4, (ng, ngs.at[me], ws_sem.at[0, 6], w_sem.at[me, 6]))
    remote = [
        pltpu.make_async_remote_copy(
            src_ref=s, dst_ref=d, send_sem=a, recv_sem=b, device_id={"section": other}, device_id_type=MESH
        )
        for s, d, a, b in remote
    ]
    for c in remote:
        c.start()

    def column(ref, k):
        return jnp.broadcast_to(ref[k : k + 1, :], (CHUNK, CHUNK)).T

    def hot(col, width, base):
        rows = col.shape[0]
        parts = []
        for q in range(width // CHUNK):
            lanes = lax.broadcasted_iota(jnp.int32, (rows, CHUNK), 1) + (base + q * CHUNK)
            parts.append(jnp.where(col == lanes, 1.0, 0.0).astype(jnp.bfloat16))
        return jnp.concatenate(parts, axis=1)

    pick[pl.ds(0, HALO), :] = hot(column(upw, 0), NV, 0)
    pick[pl.ds(HALO, HALO), :] = hot(column(dnw, 0), NV, 0)

    def halo_copies(l):
        return [
            pltpu.make_async_remote_copy(
                src_ref=sendbuf.at[l, pl.ds(q * HALO, HALO)],
                dst_ref=halo.at[l, pl.ds(q * HALO, HALO)],
                send_sem=h_send.at[l, q],
                recv_sem=h_recv.at[l, q],
                device_id={"node": target},
                device_id_type=MESH,
            )
            for q, target in enumerate((above, below))
        ]

    def send_halo(l):
        sendbuf[l] = dot(pick[...], nodes[...]).astype(jnp.bfloat16)
        for c in halo_copies(l):
            c.start()

    copy_nodes.wait()
    send_halo(0)

    live = count[0]
    for k in range(E // CHUNK):
        rows = pl.ds(k * CHUNK, CHUNK)
        x[rows, pl.ds(LOC, NV + 2 * HALO)] = hot(column(snd, k), NV + 2 * HALO, 0)
        x[rows, pl.ds(REC, NV)] = hot(column(rcv, k), NV, 0)
        slot = lax.broadcasted_iota(jnp.int32, (NV, CHUNK), 1) + k * CHUNK
        node = lax.broadcasted_iota(jnp.int32, (NV, CHUNK), 0)
        row = jnp.broadcast_to(rcv[k : k + 1, :], (NV, CHUNK))
        oht[:, rows] = jnp.where((row == node) & (slot < live), 1.0, 0.0).astype(jnp.bfloat16)

    copy_edges.wait()

    def arrived(l, p, ref):
        pltpu.make_async_copy(ref, ref, w_sem.at[l, p]).wait()

    def layer(l, carry):
        sec = l // OWN
        sub = lax.rem(l, OWN)

        @pl.when(sub == 0)
        def _():
            arrived(sec, 5, egs.at[sec])
            arrived(sec, 6, ngs.at[sec])

        arrived(l, 0, w23.at[l])
        wcat[l, pl.ds(D, NV), :] = dot(nodes[...], w23[l, pl.ds(D, D), :]).astype(jnp.bfloat16)
        wcat[l, pl.ds(LOC, NV), :] = dot(nodes[...], w23[l, pl.ds(0, D), :]).astype(jnp.bfloat16)
        arrived(l, 1, wcat.at[l, pl.ds(0, D)])
        for t in range(E // TILE):
            rows = pl.ds(t * TILE, TILE)
            pre[rows, :] = dot(x[rows, pl.ds(0, HAL)], wcat[l, pl.ds(0, HAL), :])
        arrived(l, 3, ni.at[l])
        pre_node[...] = dot(nodes[...], ni[l, pl.ds(0, D), :])

        for c in halo_copies(l):
            c.wait_recv()
        wcat[l, pl.ds(HAL, 2 * HALO), :] = dot(halo[l], w23[l, pl.ds(0, D), :]).astype(jnp.bfloat16)
        arrived(l, 2, wo.at[l])
        gain = egs[sec, pl.ds(sub, 1), :]
        for t in range(E // TILE):
            rows = pl.ds(t * TILE, TILE)
            full = pre[rows, :] + dot(x[rows, pl.ds(HAL, 2 * HALO)], wcat[l, pl.ds(HAL, 2 * HALO), :])
            update = dot(silu(full).astype(jnp.bfloat16), wo[l])
            x[rows, pl.ds(0, D)] = residual_norm(x[rows, pl.ds(0, D)], update, gain)
        aggregate = dot(oht[...], x[:, pl.ds(0, D)]).astype(jnp.bfloat16)

        arrived(l, 4, no.at[l])
        hidden = silu(pre_node[...] + dot(aggregate, ni[l, pl.ds(D, D), :])).astype(jnp.bfloat16)
        nodes[...] = residual_norm(nodes[...], dot(hidden, no[l]), ngs[sec, pl.ds(sub, 1), :])

        @pl.when(l < L - 1)
        def _():
            send_halo(l + 1)

        return carry

    lax.fori_loop(0, L, layer, 0)
    out[0] = nodes[...]

    for c in remote:
        c.wait_send()
    for l in range(L):
        for c in halo_copies(l):
            c.wait_send()


def on_device(node_latents, edge_latents, sender, receiver, send_up, send_down, edge_count, wei, weo, eg, wni, wno, ng):
    n_node = lax.axis_size("node")
    vmem = pl.BlockSpec(memory_space=pltpu.VMEM)
    smem = pl.BlockSpec(memory_space=pltpu.SMEM)
    hbm = pl.BlockSpec(memory_space=pl.ANY)
    bf16, f32 = jnp.bfloat16, jnp.float32
    return pl.pallas_call(
        functools.partial(kernel, n_node),
        out_shape=jax.ShapeDtypeStruct((1, NV, D), bf16),
        in_specs=[hbm, hbm, vmem, vmem, vmem, vmem, smem, hbm, hbm, hbm, hbm, hbm, hbm],
        out_specs=vmem,
        scratch_shapes=[
            pltpu.VMEM((NV, D), bf16),
            pltpu.VMEM((E, XW), bf16),
            pltpu.VMEM((E, D), f32),
            pltpu.VMEM((NV, E), bf16),
            pltpu.VMEM((2 * HALO, NV), bf16),
            pltpu.VMEM((L, XW, D), bf16),
            pltpu.VMEM((L, 2 * D, D), bf16),
            pltpu.VMEM((L, D, D), bf16),
            pltpu.VMEM((L, 2 * D, D), bf16),
            pltpu.VMEM((L, D, D), bf16),
            pltpu.VMEM((2, OWN, D), f32),
            pltpu.VMEM((2, OWN, D), f32),
            pltpu.VMEM((L, 2 * HALO, D), bf16),
            pltpu.VMEM((L, 2 * HALO, D), bf16),
            pltpu.VMEM((NV, D), f32),
            pltpu.SemaphoreType.DMA((2,)),
            pltpu.SemaphoreType.DMA((L, 7)),
            pltpu.SemaphoreType.DMA((OWN, 7)),
            pltpu.SemaphoreType.DMA((L, 2)),
            pltpu.SemaphoreType.DMA((L, 2)),
        ],
        compiler_params=pltpu.CompilerParams(
            collective_id=0, has_side_effects=True, vmem_limit_bytes=56 * 1024 * 1024
        ),
        cost_estimate=pl.CostEstimate(
            flops=2 * L * 5 * E * D * D, bytes_accessed=18 * 1024 * 1024, transcendentals=L * E * D
        ),
    )(
        node_latents,
        edge_latents,
        sender.reshape(E // CHUNK, CHUNK),
        receiver.reshape(E // CHUNK, CHUNK),
        send_up.reshape(1, HALO),
        send_down.reshape(1, HALO),
        edge_count,
        wei,
        weo,
        eg,
        wni,
        wno,
        ng,
    )


def solution(mesh):
    return jax.shard_map(
        on_device,
        mesh=mesh,
        in_specs=(
            P(None, "node", None),
            P(None, "node", None),
            P("node"),
            P("node"),
            P("node"),
            P("node"),
            P("node"),
            P("section", None, None),
            P("section", None, None),
            P("section", None),
            P("section", None, None),
            P("section", None, None),
            P("section", None),
        ),
        out_specs=P("section", "node", None),
        check_vma=False,
    )
```

profile of v0, /device:TPU:0, one launch (start us, length us, event | category | flops | bytes accessed | tf_op | source)
XLA Modules:
  0.0 56.3 jit_solution(6774552943113044043)
XLA Ops:
  0.7 54.0 %shard_map.127 = bf16[1,256,512]{2,1,0:T(8,128)(2,1)} custom-call(bf16[2,256,512]{2,1,0:T(8,128)(2,1)} %node_in.1, bf16[2,1536,512]{2,1,0:T(8,128)(2,1)} %edge_in.1, s32[12,128]{1,0:T(8,128)} %bitcast.4, s32[12,128]{1,0:T(8,128)} %bitcast.5, s32[1,128]{1,0:T(1,128)} %bitcast.6, s32[1,128]{1,0:T(1,128)} %bitcast.7, s32[1]{0:T(128)S(6)} %copy.15.count, ...), custom_call_target="tpu_custom_call" | custom-call | flops 16106127360 | bytes 18874368 | tf_op jit(solution)/shard_map/pallas_call | solution.py:238
  54.7 1.7 %copy.16 = bf16[1,256,512]{2,1,0:T(8,128)(2,1)} copy(bf16[1,256,512]{2,1,0:T(8,128)(2,1)} %shard_map.127) | data formatting | bytes 524288
where the time goes:
time: 56.5 us; the launch traced here: 56.3 us
  Pallas kernels  54 us (96%)
  local copies, waits for them, and re-layouts  1.67 us (3%)
  between operations  0.66 us (1%)
    pallas_call x1, Pallas kernels, on_device(): pl.pallas_call(functools.partial(kernel, n_node), out_shape=jax.ShapeDtyp...  54 us
    unnamed x1, local copies, waits for them, and re-layouts  1.67 us

commit v1 on v0

--- a/solution.py
+++ b/solution.py
@@ -14,6 +14,7 @@
 L = 4
 OWN = 2
 TILE = 256
+BTILE = 256
 CHUNK = 128
 MESH = pl.DeviceIdType.MESH
 
@@ -23,16 +24,22 @@
 XW = HAL + 2 * HALO
 
 
-def silu(x):
-    half = 0.5 * x
-    return half + half * jnp.tanh(half)
+def silu_of_half(half):
+    return (half + half * jnp.tanh(half)).astype(jnp.bfloat16)
+
+
+def centred(weight):
+    weight = weight.astype(jnp.float32)
+    return (weight - jnp.mean(weight, axis=-1, keepdims=True)).astype(jnp.bfloat16)
 
 
 def residual_norm(base, update, gain):
-    mean = jnp.mean(update, axis=-1, keepdims=True)
-    centred = update - mean
-    var = jnp.mean(centred * centred, axis=-1, keepdims=True)
-    return (base.astype(jnp.float32) + gain * (centred * lax.rsqrt(var + 1e-05))).astype(jnp.bfloat16)
+    scale = lax.rsqrt(jnp.mean(update * update, axis=-1, keepdims=True) + 1e-05)
+    return (base.astype(jnp.float32) + (update * scale) * gain).astype(jnp.bfloat16)
+
+
+def halved(value):
+    return (0.5 * value.astype(jnp.float32)).astype(jnp.bfloat16)
 
 
 def dot(a, b):
@@ -43,11 +50,11 @@
     n_node,
     node_in,
     edge_in,
-    snd,
-    rcv,
-    upw,
-    dnw,
-    count,
+    snd_in,
+    rcv_in,
+    up_in,
+    dn_in,
+    count_in,
     wei,
     weo,
     eg,
@@ -55,9 +62,15 @@
     wno,
     ng,
     out,
+    snd,
+    rcv,
+    upw,
+    dnw,
+    count,
     nodes,
     x,
     pre,
+    hid,
     oht,
     pick,
     wcat,
@@ -83,7 +96,17 @@
     below = lax.rem(at + n_node - 1, n_node)
 
     copy_nodes = pltpu.make_async_copy(node_in.at[me], nodes, in_sem.at[0])
-    copy_nodes.start()
+    copy_picks = [
+        pltpu.make_async_copy(up_in, upw, in_sem.at[2]),
+        pltpu.make_async_copy(dn_in, dnw, in_sem.at[3]),
+    ]
+    copy_ends = [
+        pltpu.make_async_copy(snd_in, snd, in_sem.at[4]),
+        pltpu.make_async_copy(rcv_in, rcv, in_sem.at[5]),
+        pltpu.make_async_copy(count_in, count, in_sem.at[6]),
+    ]
+    for c in copy_picks + [copy_nodes] + copy_ends:
+        c.start()
 
     def pieces(j):
         k = OWN * me + j
@@ -101,17 +124,17 @@
             own.append(pltpu.make_async_copy(src, dst, w_sem.at[OWN * me + j, p]))
     own.append(pltpu.make_async_copy(eg, egs.at[me], w_sem.at[me, 5]))
     own.append(pltpu.make_async_copy(ng, ngs.at[me], w_sem.at[me, 6]))
-    for c in own[:5]:
+    first = own[:5] + own[10:]
+    for c in first[:2]:
         c.start()
     copy_edges = pltpu.make_async_copy(edge_in.at[me], x.at[:, pl.ds(0, D)], in_sem.at[1])
     copy_edges.start()
-    for c in own[5:]:
+    for c in first[2:]:
         c.start()
 
     barrier = pltpu.get_barrier_semaphore()
     for target in ({"section": other}, {"node": above}, {"node": below}):
         pl.semaphore_signal(barrier, inc=1, device_id=target, device_id_type=MESH)
-    pl.semaphore_wait(barrier, 3)
 
     remote = []
     for j in range(OWN):
@@ -125,8 +148,6 @@
         )
         for s, d, a, b in remote
     ]
-    for c in remote:
-        c.start()
 
     def column(ref, k):
         return jnp.broadcast_to(ref[k : k + 1, :], (CHUNK, CHUNK)).T
@@ -139,6 +160,8 @@
             parts.append(jnp.where(col == lanes, 1.0, 0.0).astype(jnp.bfloat16))
         return jnp.concatenate(parts, axis=1)
 
+    for c in copy_picks:
+        c.wait()
     pick[pl.ds(0, HALO), :] = hot(column(upw, 0), NV, 0)
     pick[pl.ds(HALO, HALO), :] = hot(column(dnw, 0), NV, 0)
 
@@ -161,8 +184,13 @@
             c.start()
 
     copy_nodes.wait()
-    send_halo(0)
-
+    sendbuf[0] = dot(pick[...], nodes[...]).astype(jnp.bfloat16)
+    pl.semaphore_wait(barrier, 3)
+    for c in halo_copies(0) + remote[:7]:
+        c.start()
+
+    for c in copy_ends:
+        c.wait()
     live = count[0]
     for k in range(E // CHUNK):
         rows = pl.ds(k * CHUNK, CHUNK)
@@ -173,6 +201,8 @@
         row = jnp.broadcast_to(rcv[k : k + 1, :], (NV, CHUNK))
         oht[:, rows] = jnp.where((row == node) & (slot < live), 1.0, 0.0).astype(jnp.bfloat16)
 
+    for c in own[5:10] + remote[7:]:
+        c.start()
     copy_edges.wait()
 
     def arrived(l, p, ref):
@@ -188,29 +218,45 @@
             arrived(sec, 6, ngs.at[sec])
 
         arrived(l, 0, w23.at[l])
-        wcat[l, pl.ds(D, NV), :] = dot(nodes[...], w23[l, pl.ds(D, D), :]).astype(jnp.bfloat16)
-        wcat[l, pl.ds(LOC, NV), :] = dot(nodes[...], w23[l, pl.ds(0, D), :]).astype(jnp.bfloat16)
+        wcat[l, pl.ds(D, NV), :] = halved(dot(nodes[...], w23[l, pl.ds(D, D), :]))
+        wcat[l, pl.ds(LOC, NV), :] = halved(dot(nodes[...], w23[l, pl.ds(0, D), :]))
         arrived(l, 1, wcat.at[l, pl.ds(0, D)])
+        wcat[l, pl.ds(0, D), :] = halved(wcat[l, pl.ds(0, D), :])
         for t in range(E // TILE):
             rows = pl.ds(t * TILE, TILE)
             pre[rows, :] = dot(x[rows, pl.ds(0, HAL)], wcat[l, pl.ds(0, HAL), :])
+        arrived(l, 2, wo.at[l])
+        wo[l] = centred(wo[l])
         arrived(l, 3, ni.at[l])
+        ni[l] = halved(ni[l])
+        arrived(l, 4, no.at[l])
+        no[l] = centred(no[l])
         pre_node[...] = dot(nodes[...], ni[l, pl.ds(0, D), :])
 
         for c in halo_copies(l):
             c.wait_recv()
-        wcat[l, pl.ds(HAL, 2 * HALO), :] = dot(halo[l], w23[l, pl.ds(0, D), :]).astype(jnp.bfloat16)
-        arrived(l, 2, wo.at[l])
+        wcat[l, pl.ds(HAL, 2 * HALO), :] = halved(dot(halo[l], w23[l, pl.ds(0, D), :]))
         gain = egs[sec, pl.ds(sub, 1), :]
-        for t in range(E // TILE):
-            rows = pl.ds(t * TILE, TILE)
+        tiles = [pl.ds(t * BTILE, BTILE) for t in range(E // BTILE)]
+
+        def stage1(rows):
             full = pre[rows, :] + dot(x[rows, pl.ds(HAL, 2 * HALO)], wcat[l, pl.ds(HAL, 2 * HALO), :])
-            update = dot(silu(full).astype(jnp.bfloat16), wo[l])
-            x[rows, pl.ds(0, D)] = residual_norm(x[rows, pl.ds(0, D)], update, gain)
+            hid[rows, :] = silu_of_half(full)
+
+        def stage2(rows):
+            pre[rows, :] = dot(hid[rows, :], wo[l])
+
+        def stage3(rows):
+            x[rows, pl.ds(0, D)] = residual_norm(x[rows, pl.ds(0, D)], pre[rows, :], gain)
+
+        stages = (stage1, stage2, stage3)
+        for step in range(len(tiles) + len(stages) - 1):
+            for k, stage in enumerate(stages):
+                if 0 <= step - k < len(tiles):
+                    stage(tiles[step - k])
         aggregate = dot(oht[...], x[:, pl.ds(0, D)]).astype(jnp.bfloat16)
 
-        arrived(l, 4, no.at[l])
-        hidden = silu(pre_node[...] + dot(aggregate, ni[l, pl.ds(D, D), :])).astype(jnp.bfloat16)
+        hidden = silu_of_half(pre_node[...] + dot(aggregate, ni[l, pl.ds(D, D), :]))
         nodes[...] = residual_norm(nodes[...], dot(hidden, no[l]), ngs[sec, pl.ds(sub, 1), :])
 
         @pl.when(l < L - 1)
@@ -232,18 +278,23 @@
 def on_device(node_latents, edge_latents, sender, receiver, send_up, send_down, edge_count, wei, weo, eg, wni, wno, ng):
     n_node = lax.axis_size("node")
     vmem = pl.BlockSpec(memory_space=pltpu.VMEM)
-    smem = pl.BlockSpec(memory_space=pltpu.SMEM)
     hbm = pl.BlockSpec(memory_space=pl.ANY)
     bf16, f32 = jnp.bfloat16, jnp.float32
     return pl.pallas_call(
         functools.partial(kernel, n_node),
         out_shape=jax.ShapeDtypeStruct((1, NV, D), bf16),
-        in_specs=[hbm, hbm, vmem, vmem, vmem, vmem, smem, hbm, hbm, hbm, hbm, hbm, hbm],
+        in_specs=[hbm, hbm, hbm, hbm, hbm, hbm, hbm, hbm, hbm, hbm, hbm, hbm, hbm],
         out_specs=vmem,
         scratch_shapes=[
+            pltpu.VMEM((E // CHUNK, CHUNK), jnp.int32),
+            pltpu.VMEM((E // CHUNK, CHUNK), jnp.int32),
+            pltpu.VMEM((1, HALO), jnp.int32),
+            pltpu.VMEM((1, HALO), jnp.int32),
+            pltpu.SMEM((1,), jnp.int32),
             pltpu.VMEM((NV, D), bf16),
             pltpu.VMEM((E, XW), bf16),
             pltpu.VMEM((E, D), f32),
+            pltpu.VMEM((E, D), bf16),
             pltpu.VMEM((NV, E), bf16),
             pltpu.VMEM((2 * HALO, NV), bf16),
             pltpu.VMEM((L, XW, D), bf16),
@@ -256,7 +307,7 @@
             pltpu.VMEM((L, 2 * HALO, D), bf16),
             pltpu.VMEM((L, 2 * HALO, D), bf16),
             pltpu.VMEM((NV, D), f32),
-            pltpu.SemaphoreType.DMA((2,)),
+            pltpu.SemaphoreType.DMA((7,)),
             pltpu.SemaphoreType.DMA((L, 7)),
             pltpu.SemaphoreType.DMA((OWN, 7)),
             pltpu.SemaphoreType.DMA((L, 2)),

time: 56.5 us -> 51.5 us (0.912)
  Pallas kernels: 54 us -> 49.1 us
    pallas_call x1, Pallas kernels: 54 us -> 49.1 us  [on_device(): pl.pallas_call(functools.partial(kernel, n_node), out_shape=jax.ShapeDtyp...]
where the time goes in v1:
time: 51.5 us; the launch traced here: 51.4 us
  Pallas kernels  49.1 us (95%)
  local copies, waits for them, and re-layouts  1.67 us (3%)
  between operations  0.66 us (1%)
    pallas_call x1, Pallas kernels, on_device(): pl.pallas_call(functools.partial(kernel, n_node), out_shape=jax.ShapeDtyp...  49.1 us
    unnamed x1, local copies, waits for them, and re-layouts  1.67 us

profile of v1, /device:TPU:0, one launch (start us, length us, event | category | flops | bytes accessed | tf_op | source)
XLA Modules:
  0.0 51.4 jit_solution(3244111637728378757)
XLA Ops:
  0.7 49.1 %shard_map.127 = bf16[1,256,512]{2,1,0:T(8,128)(2,1)} custom-call(bf16[2,256,512]{2,1,0:T(8,128)(2,1)} %node_in.1, bf16[2,1536,512]{2,1,0:T(8,128)(2,1)} %edge_in.1, s32[12,128]{1,0:T(8,128)} %bitcast.4, s32[12,128]{1,0:T(8,128)} %bitcast.5, s32[1,128]{1,0:T(1,128)} %bitcast.6, s32[1,128]{1,0:T(1,128)} %bitcast.7, s32[1]{0:T(128)S(6)} %copy.15.count_in, ...), custom_call_target="tpu_custom_call" | custom-call | flops 16106127360 | bytes 18874368 | tf_op jit(solution)/shard_map/pallas_call | solution.py:283
  49.7 1.7 %copy.16 = bf16[1,256,512]{2,1,0:T(8,128)(2,1)} copy(bf16[1,256,512]{2,1,0:T(8,128)(2,1)} %shard_map.127) | data formatting | bytes 524288

commit v2 on v1

--- a/solution.py
+++ b/solution.py
@@ -95,6 +95,10 @@
     above = lax.rem(at + 1, n_node)
     below = lax.rem(at + n_node - 1, n_node)
 
+    barrier = pltpu.get_barrier_semaphore()
+    for target in ({"section": other}, {"node": above}, {"node": below}):
+        pl.semaphore_signal(barrier, inc=1, device_id=target, device_id_type=MESH)
+
     copy_nodes = pltpu.make_async_copy(node_in.at[me], nodes, in_sem.at[0])
     copy_picks = [
         pltpu.make_async_copy(up_in, upw, in_sem.at[2]),
@@ -132,9 +136,6 @@
     for c in first[2:]:
         c.start()
 
-    barrier = pltpu.get_barrier_semaphore()
-    for target in ({"section": other}, {"node": above}, {"node": below}):
-        pl.semaphore_signal(barrier, inc=1, device_id=target, device_id_type=MESH)
 
     remote = []
     for j in range(OWN):
@@ -282,7 +283,7 @@
     bf16, f32 = jnp.bfloat16, jnp.float32
     return pl.pallas_call(
         functools.partial(kernel, n_node),
-        out_shape=jax.ShapeDtypeStruct((1, NV, D), bf16),
+        out_shape=pltpu.VMEM((1, NV, D), bf16),
         in_specs=[hbm, hbm, hbm, hbm, hbm, hbm, hbm, hbm, hbm, hbm, hbm, hbm, hbm],
         out_specs=vmem,
         scratch_shapes=[

time: 51.5 us -> 49.8 us (0.967)
  local copies, waits for them, and re-layouts: 1.67 us -> 0.71 us
  Pallas kernels: 49.1 us -> 48.3 us
    unnamed x1, local copies, waits for them, and re-layouts: 1.67 us -> 0.71 us
    pallas_call x1, Pallas kernels: 49.1 us -> 48.3 us  [on_device(): pl.pallas_call(functools.partial(kernel, n_node), out_shape=pltpu.VMEM((1...]
where the time goes in v2:
time: 49.8 us; the launch traced here: 49.7 us
  Pallas kernels  48.3 us (97%)
  local copies, waits for them, and re-layouts  0.71 us (1%)
  between operations  0.66 us (1%)
    pallas_call x1, Pallas kernels, on_device(): pl.pallas_call(functools.partial(kernel, n_node), out_shape=pltpu.VMEM((1...  48.3 us

profile of v2, /device:TPU:0, one launch (start us, length us, event | category | flops | bytes accessed | tf_op | source)
XLA Modules:
  0.0 49.7 jit_solution(17676640550630367624)
XLA Ops:
  0.7 48.3 %shard_map.127 = bf16[1,256,512]{2,1,0:T(8,128)(2,1)S(1)} custom-call(bf16[2,256,512]{2,1,0:T(8,128)(2,1)} %node_in.1, bf16[2,1536,512]{2,1,0:T(8,128)(2,1)} %edge_in.1, s32[12,128]{1,0:T(8,128)} %bitcast.4, s32[12,128]{1,0:T(8,128)} %bitcast.5, s32[1,128]{1,0:T(1,128)} %bitcast.6, s32[1,128]{1,0:T(1,128)} %bitcast.7, s32[1]{0:T(128)S(6)} %copy.16.count_in, ...), custom_call_target="tpu_custom_call" | custom-call | flops 16106127360 | bytes 18874368 | tf_op jit(solution)/shard_map/pallas_call | solution.py:284
  49.0 0.7 %copy.15 = bf16[1,256,512]{2,1,0:T(8,128)(2,1)} copy(bf16[1,256,512]{2,1,0:T(8,128)(2,1)S(1)} %shard_map.127) | data formatting | bytes 524288

commit v3 on v2

--- a/solution.py
+++ b/solution.py
@@ -16,6 +16,7 @@
 TILE = 256
 BTILE = 256
 CHUNK = 128
+PART = HALO // 2
 MESH = pl.DeviceIdType.MESH
 
 REC = D
@@ -72,6 +73,7 @@
     pre,
     hid,
     oht,
+    ohts,
     pick,
     wcat,
     w23,
@@ -83,6 +85,7 @@
     halo,
     sendbuf,
     pre_node,
+    pre_sent,
     in_sem,
     w_sem,
     ws_sem,
@@ -163,31 +166,31 @@
 
     for c in copy_picks:
         c.wait()
-    pick[pl.ds(0, HALO), :] = hot(column(upw, 0), NV, 0)
-    pick[pl.ds(HALO, HALO), :] = hot(column(dnw, 0), NV, 0)
-
-    def halo_copies(l):
+    sent_up, sent_down = column(upw, 0), column(dnw, 0)
+    sent = [jnp.concatenate([c[h * PART : (h + 1) * PART] for c in (sent_up, sent_down)], axis=0) for h in range(2)]
+    for h in range(2):
+        pick[pl.ds(h * HALO, HALO), :] = hot(sent[h], NV, 0)
+
+    def halo_copies(l, h):
         return [
             pltpu.make_async_remote_copy(
-                src_ref=sendbuf.at[l, pl.ds(q * HALO, HALO)],
-                dst_ref=halo.at[l, pl.ds(q * HALO, HALO)],
-                send_sem=h_send.at[l, q],
-                recv_sem=h_recv.at[l, q],
+                src_ref=sendbuf.at[l, pl.ds((2 * h + q) * PART, PART)],
+                dst_ref=halo.at[l, pl.ds(q * HALO + h * PART, PART)],
+                send_sem=h_send.at[l, h, q],
+                recv_sem=h_recv.at[l, h, q],
                 device_id={"node": target},
                 device_id_type=MESH,
             )
             for q, target in enumerate((above, below))
         ]
 
-    def send_halo(l):
-        sendbuf[l] = dot(pick[...], nodes[...]).astype(jnp.bfloat16)
-        for c in halo_copies(l):
-            c.start()
+    def all_halo_copies(l):
+        return halo_copies(l, 0) + halo_copies(l, 1)
 
     copy_nodes.wait()
     sendbuf[0] = dot(pick[...], nodes[...]).astype(jnp.bfloat16)
     pl.semaphore_wait(barrier, 3)
-    for c in halo_copies(0) + remote[:7]:
+    for c in all_halo_copies(0) + remote[:7]:
         c.start()
 
     for c in copy_ends:
@@ -201,6 +204,10 @@
         node = lax.broadcasted_iota(jnp.int32, (NV, CHUNK), 0)
         row = jnp.broadcast_to(rcv[k : k + 1, :], (NV, CHUNK))
         oht[:, rows] = jnp.where((row == node) & (slot < live), 1.0, 0.0).astype(jnp.bfloat16)
+        for h in range(2):
+            ohts[pl.ds(h * HALO, HALO), rows] = jnp.where(
+                (row[:HALO] == sent[h]) & (slot[:HALO] < live), 1.0, 0.0
+            ).astype(jnp.bfloat16)
 
     for c in own[5:10] + remote[7:]:
         c.start()
@@ -209,14 +216,16 @@
     def arrived(l, p, ref):
         pltpu.make_async_copy(ref, ref, w_sem.at[l, p]).wait()
 
-    def layer(l, carry):
+    def layer(l, last):
         sec = l // OWN
-        sub = lax.rem(l, OWN)
-
-        @pl.when(sub == 0)
-        def _():
-            arrived(sec, 5, egs.at[sec])
-            arrived(sec, 6, ngs.at[sec])
+        sub = l % OWN
+
+        if not last:
+
+            @pl.when(sub == 0)
+            def _():
+                arrived(sec, 5, egs.at[sec])
+                arrived(sec, 6, ngs.at[sec])
 
         arrived(l, 0, w23.at[l])
         wcat[l, pl.ds(D, NV), :] = halved(dot(nodes[...], w23[l, pl.ds(D, D), :]))
@@ -233,8 +242,10 @@
         arrived(l, 4, no.at[l])
         no[l] = centred(no[l])
         pre_node[...] = dot(nodes[...], ni[l, pl.ds(0, D), :])
-
-        for c in halo_copies(l):
+        if not last:
+            pre_sent[...] = dot(sendbuf[l], ni[l, pl.ds(0, D), :])
+
+        for c in all_halo_copies(l):
             c.wait_recv()
         wcat[l, pl.ds(HAL, 2 * HALO), :] = halved(dot(halo[l], w23[l, pl.ds(0, D), :]))
         gain = egs[sec, pl.ds(sub, 1), :]
@@ -255,24 +266,37 @@
             for k, stage in enumerate(stages):
                 if 0 <= step - k < len(tiles):
                     stage(tiles[step - k])
+        node_gain = ngs[sec, pl.ds(sub, 1), :]
+
+        def hidden_of(aggregate, pre_act):
+            return silu_of_half(pre_act + dot(aggregate, ni[l, pl.ds(D, D), :]))
+
+        if not last:
+            aggregate = dot(ohts[...], x[:, pl.ds(0, D)]).astype(jnp.bfloat16)
+            parts = [pl.ds(h * HALO, HALO) for h in range(2)]
+            hidden = [hidden_of(aggregate[h * HALO : (h + 1) * HALO], pre_sent[parts[h], :]) for h in range(2)]
+            for h in range(2):
+                new = residual_norm(sendbuf[l, parts[h], :], dot(hidden[h], no[l]), node_gain)
+                sendbuf[l + 1, parts[h], :] = new
+                for c in halo_copies(l + 1, h):
+                    c.start()
+
         aggregate = dot(oht[...], x[:, pl.ds(0, D)]).astype(jnp.bfloat16)
-
-        hidden = silu_of_half(pre_node[...] + dot(aggregate, ni[l, pl.ds(D, D), :]))
-        nodes[...] = residual_norm(nodes[...], dot(hidden, no[l]), ngs[sec, pl.ds(sub, 1), :])
-
-        @pl.when(l < L - 1)
-        def _():
-            send_halo(l + 1)
-
+        hidden = hidden_of(aggregate, pre_node[...])
+        nodes[...] = residual_norm(nodes[...], dot(hidden, no[l]), node_gain)
+
+    def step(l, carry):
+        layer(l, False)
         return carry
 
-    lax.fori_loop(0, L, layer, 0)
+    lax.fori_loop(0, L - 1, step, 0)
+    layer(L - 1, True)
     out[0] = nodes[...]
 
     for c in remote:
         c.wait_send()
     for l in range(L):
-        for c in halo_copies(l):
+        for c in all_halo_copies(l):
             c.wait_send()
 
 
@@ -297,6 +321,7 @@
             pltpu.VMEM((E, D), f32),
             pltpu.VMEM((E, D), bf16),
             pltpu.VMEM((NV, E), bf16),
+            pltpu.VMEM((2 * HALO, E), bf16),
             pltpu.VMEM((2 * HALO, NV), bf16),
             pltpu.VMEM((L, XW, D), bf16),
             pltpu.VMEM((L, 2 * D, D), bf16),
@@ -308,11 +333,12 @@
             pltpu.VMEM((L, 2 * HALO, D), bf16),
             pltpu.VMEM((L, 2 * HALO, D), bf16),
             pltpu.VMEM((NV, D), f32),
+            pltpu.VMEM((2 * HALO, D), f32),
             pltpu.SemaphoreType.DMA((7,)),
             pltpu.SemaphoreType.DMA((L, 7)),
             pltpu.SemaphoreType.DMA((OWN, 7)),
-            pltpu.SemaphoreType.DMA((L, 2)),
-            pltpu.SemaphoreType.DMA((L, 2)),
+            pltpu.SemaphoreType.DMA((L, 2, 2)),
+            pltpu.SemaphoreType.DMA((L, 2, 2)),
         ],
         compiler_params=pltpu.CompilerParams(
             collective_id=0, has_side_effects=True, vmem_limit_bytes=56 * 1024 * 1024

time: 49.8 us -> 48.8 us (0.980)
  Pallas kernels: 48.3 us -> 47.3 us
    pallas_call x1, Pallas kernels: 48.3 us -> 47.3 us  [on_device(): pl.pallas_call(functools.partial(kernel, n_node), out_shape=pltpu.VMEM((1...]
where the time goes in v3:
time: 48.8 us; the launch traced here: 48.7 us
  Pallas kernels  47.3 us (97%)
  local copies, waits for them, and re-layouts  0.71 us (1%)
  between operations  0.66 us (1%)
    pallas_call x1, Pallas kernels, on_device(): pl.pallas_call(functools.partial(kernel, n_node), out_shape=pltpu.VMEM((1...  47.3 us

profile of v3, /device:TPU:0, one launch (start us, length us, event | category | flops | bytes accessed | tf_op | source)
XLA Modules:
  0.0 48.7 jit_solution(13679607191509031210)
XLA Ops:
  0.7 47.3 %shard_map.127 = bf16[1,256,512]{2,1,0:T(8,128)(2,1)S(1)} custom-call(bf16[2,256,512]{2,1,0:T(8,128)(2,1)} %node_in.1, bf16[2,1536,512]{2,1,0:T(8,128)(2,1)} %edge_in.1, s32[12,128]{1,0:T(8,128)} %bitcast.4, s32[12,128]{1,0:T(8,128)} %bitcast.5, s32[1,128]{1,0:T(1,128)} %bitcast.6, s32[1,128]{1,0:T(1,128)} %bitcast.7, s32[1]{0:T(128)S(6)} %copy.16.count_in, ...), custom_call_target="tpu_custom_call" | custom-call | flops 16106127360 | bytes 18874368 | tf_op jit(solution)/shard_map/pallas_call | solution.py:308
  47.9 0.7 %copy.15 = bf16[1,256,512]{2,1,0:T(8,128)(2,1)} copy(bf16[1,256,512]{2,1,0:T(8,128)(2,1)S(1)} %shard_map.127) | data formatting | bytes 524288

commit v4 on v3

--- a/solution.py
+++ b/solution.py
@@ -84,6 +84,8 @@
     ngs,
     halo,
     sendbuf,
+    nodes_cross,
+    crossbuf,
     pre_node,
     pre_sent,
     in_sem,
@@ -99,7 +101,8 @@
     below = lax.rem(at + n_node - 1, n_node)
 
     barrier = pltpu.get_barrier_semaphore()
-    for target in ({"section": other}, {"node": above}, {"node": below}):
+    targets = [{"section": other}] + [{"section": c, "node": n} for c in (me, other) for n in (above, below)]
+    for target in targets:
         pl.semaphore_signal(barrier, inc=1, device_id=target, device_id_type=MESH)
 
     copy_nodes = pltpu.make_async_copy(node_in.at[me], nodes, in_sem.at[0])
@@ -112,7 +115,8 @@
         pltpu.make_async_copy(rcv_in, rcv, in_sem.at[5]),
         pltpu.make_async_copy(count_in, count, in_sem.at[6]),
     ]
-    for c in copy_picks + [copy_nodes] + copy_ends:
+    copy_cross = pltpu.make_async_copy(node_in.at[other], nodes_cross, in_sem.at[7])
+    for c in copy_picks + [copy_cross, copy_nodes] + copy_ends:
         c.start()
 
     def pieces(j):
@@ -187,11 +191,25 @@
     def all_halo_copies(l):
         return halo_copies(l, 0) + halo_copies(l, 1)
 
+    copy_cross.wait()
+    crossbuf[...] = dot(pick[...], nodes_cross[...]).astype(jnp.bfloat16)
+    pl.semaphore_wait(barrier, 5)
+    cross = [
+        pltpu.make_async_remote_copy(
+            src_ref=crossbuf.at[pl.ds((2 * h + q) * PART, PART)],
+            dst_ref=halo.at[0, pl.ds(q * HALO + h * PART, PART)],
+            send_sem=h_send.at[0, h, q],
+            recv_sem=h_recv.at[0, h, q],
+            device_id={"section": other, "node": target},
+            device_id_type=MESH,
+        )
+        for h in range(2)
+        for q, target in enumerate((above, below))
+    ]
+    for c in cross + remote[:7]:
+        c.start()
     copy_nodes.wait()
     sendbuf[0] = dot(pick[...], nodes[...]).astype(jnp.bfloat16)
-    pl.semaphore_wait(barrier, 3)
-    for c in all_halo_copies(0) + remote[:7]:
-        c.start()
 
     for c in copy_ends:
         c.wait()
@@ -332,9 +350,11 @@
             pltpu.VMEM((2, OWN, D), f32),
             pltpu.VMEM((L, 2 * HALO, D), bf16),
             pltpu.VMEM((L, 2 * HALO, D), bf16),
+            pltpu.VMEM((NV, D), bf16),
+            pltpu.VMEM((2 * HALO, D), bf16),
             pltpu.VMEM((NV, D), f32),
             pltpu.VMEM((2 * HALO, D), f32),
-            pltpu.SemaphoreType.DMA((7,)),
+            pltpu.SemaphoreType.DMA((8,)),
             pltpu.SemaphoreType.DMA((L, 7)),
             pltpu.SemaphoreType.DMA((OWN, 7)),
             pltpu.SemaphoreType.DMA((L, 2, 2)),

time: 48.8 us -> 50.4 us (1.033)
  Pallas kernels: 47.3 us -> 48.9 us
    pallas_call x1, Pallas kernels: 47.3 us -> 48.9 us  [on_device(): pl.pallas_call(functools.partial(kernel, n_node), out_shape=pltpu.VMEM((1...]
where the time goes in v4:
time: 50.4 us; the launch traced here: 50.3 us
  Pallas kernels  48.9 us (97%)
  local copies, waits for them, and re-layouts  0.71 us (1%)
  between operations  0.66 us (1%)
    pallas_call x1, Pallas kernels, on_device(): pl.pallas_call(functools.partial(kernel, n_node), out_shape=pltpu.VMEM((1...  48.9 us

profile of v4, /device:TPU:0, one launch (start us, length us, event | category | flops | bytes accessed | tf_op | source)
XLA Modules:
  0.0 50.3 jit_solution(1639510493346358792)
XLA Ops:
  0.7 48.9 %shard_map.127 = bf16[1,256,512]{2,1,0:T(8,128)(2,1)S(1)} custom-call(bf16[2,256,512]{2,1,0:T(8,128)(2,1)} %node_in.1, bf16[2,1536,512]{2,1,0:T(8,128)(2,1)} %edge_in.1, s32[12,128]{1,0:T(8,128)} %bitcast.4, s32[12,128]{1,0:T(8,128)} %bitcast.5, s32[1,128]{1,0:T(1,128)} %bitcast.6, s32[1,128]{1,0:T(1,128)} %bitcast.7, s32[1]{0:T(128)S(6)} %copy.16.count_in, ...), custom_call_target="tpu_custom_call" | custom-call | flops 16106127360 | bytes 18874368 | tf_op jit(solution)/shard_map/pallas_call | solution.py:326
  49.6 0.7 %copy.15 = bf16[1,256,512]{2,1,0:T(8,128)(2,1)} copy(bf16[1,256,512]{2,1,0:T(8,128)(2,1)S(1)} %shard_map.127) | data formatting | bytes 524288
